TPU v7x, 128 devices: a whole 4x4x4 slice. The times are simulated.
128 devices in a mesh: replica: 8 (over x_lo, y), fsdp: 16 (over z, x_hi, core).
Axes of the slice: x: 4 (x_hi: 2, x_lo: 2; x = x_hi * 2 + x_lo), y: 4, z: 4, core: 2. Of those that a mesh axis runs over, the one named last changes fastest.
Arguments:
- tokens: bfloat16 [8, 16384, 4096], P('replica', 'fsdp'), may hold values from -6 to 6
- norm_gain: float32 [4096], replicated, may hold values from 0.25 to 1.75
- value_weight: bfloat16 [8, 4096, 512], P('replica', 'fsdp'), may hold values from -0.09375 to 0.09375
- output_weight: bfloat16 [8, 4096, 512], P('replica', 'fsdp'), may hold values from -0.25 to 0.25
- out_cotangent: bfloat16 [8, 16384, 4096], P('replica', 'fsdp'), may hold values from -0.15625 to 0.15625
- base_params: bfloat16 [65536, 128], P('fsdp'), may hold values from -6 to 6
- outer_momentum: float32 [65536, 128], P('fsdp'), may hold values from -4 to 4
- delta_values: bfloat16 [8, 65536, 128], P('replica', 'fsdp'), may hold values from -8 to 8
- delta_exponents: int32 [8, 65536], P('replica', 'fsdp'), may hold values from -3 to 1
Outputs:
- value_grad: float32 [8, 4096, 512], P('replica', 'fsdp')
- output_grad: float32 [8, 4096, 512], P('replica', 'fsdp')
- new_base: bfloat16 [65536, 128], P('fsdp')
- new_momentum: float32 [65536, 128], P('fsdp')
All inputs are finite; a program needn't handle non-finite values.
Results may differ from a plain program's by a relative error of at most 0.015.
Values may be sent and summed in bfloat16 or wider, within the bound.
A program may use at most 128 MiB of HBM per device.

v0:
```python
import jax
import jax.numpy as jnp
from jax import lax
from jax.sharding import PartitionSpec as P


def nesterov(delta, base_part, momentum_part):
    momentum_next = 0.9 * momentum_part + delta
    base_next = (base_part.astype(jnp.float32) - 0.7 * (delta + 0.9 * momentum_next)).astype(
        jnp.bfloat16
    )
    return (base_next, momentum_next)


def per_device(
    tokens,
    norm_gain,
    value_weight,
    output_weight,
    out_cotangent,
    base_params,
    outer_momentum,
    delta_values,
    delta_exponents,
):
    replicas = lax.axis_size("replica")
    xf = tokens[0].astype(jnp.float32)
    scale = lax.rsqrt(jnp.mean(xf * xf, axis=1, keepdims=True) + 1e-05)
    normed = (xf * scale * norm_gain).astype(jnp.bfloat16)
    cotangent = out_cotangent[0]
    normed_cols = normed
    cot_cols = cotangent
    first = jnp.dot(
        normed_cols,
        lax.all_gather(value_weight[0], "fsdp", axis=0, tiled=True),
        preferred_element_type=jnp.float32,
    )
    second = jnp.dot(
        cot_cols,
        lax.all_gather(output_weight[0], "fsdp", axis=0, tiled=True),
        preferred_element_type=jnp.float32,
    )
    values = first.astype(jnp.bfloat16)
    value_cot = second.astype(jnp.bfloat16)
    cot_cols = cotangent
    output_grad = lax.psum_scatter(
        lax.dot_general(
            cot_cols, values, (((0,), (0,)), ((), ())), preferred_element_type=jnp.float32
        ).astype(jnp.bfloat16),
        "fsdp",
        scatter_dimension=0,
        tiled=True,
    ).astype(jnp.float32)
    normed_cols = normed
    value_grad = lax.psum_scatter(
        lax.dot_general(
            normed_cols, value_cot, (((0,), (0,)), ((), ())), preferred_element_type=jnp.float32
        ).astype(jnp.bfloat16),
        "fsdp",
        scatter_dimension=0,
        tiled=True,
    ).astype(jnp.float32)
    scaled = (
        delta_values[0].astype(jnp.float32)
        * jnp.exp2(delta_exponents[0].astype(jnp.float32))[:, None]
    )
    delta = lax.psum(scaled.astype(jnp.bfloat16), "replica").astype(jnp.float32) * (1.0 / replicas)
    new_base, new_momentum = nesterov(delta, base_params, outer_momentum)
    return (value_grad[None], output_grad[None], new_base, new_momentum)


def solution(mesh):
    return jax.shard_map(
        per_device,
        mesh=mesh,
        in_specs=(
            P("replica", "fsdp", None),
            P(),
            P("replica", "fsdp", None),
            P("replica", "fsdp", None),
            P("replica", "fsdp", None),
            P("fsdp", None),
            P("fsdp", None),
            P("replica", "fsdp", None),
            P("replica", "fsdp"),
        ),
        out_specs=(
            P("replica", "fsdp", None),
            P("replica", "fsdp", None),
            P("fsdp", None),
            P("fsdp", None),
        ),
        check_vma=False,
    )
```

profile of v0, /device:TPU:0, one launch (start us, length us, event | category | flops | bytes accessed | tf_op | source)
XLA Modules:
  0.0 301.3 jit_solution(4929289135054192510)
XLA Ops:
  8.0 0.0 all-gather.7.cloned.1.call-start
  8.0 0.7 all-gather.7.cloned.1.call-update
  8.7 0.0 all-gather.5.cloned.1.call-start
  8.8 0.7 all-gather.5.cloned.1.call-update
  9.5 0.0 all-reduce.2.cloned.1.call-start
  9.5 0.7 multiply_exponential_fusion
  10.3 2.5 fusion.18
  12.8 0.0 all-reduce.2.cloned.1.call-update
  12.8 0.0 copy-start.2
  12.9 0.0 reduce-scatter.5.cloned.1.call-start
  12.9 5.1 %fusion = f32[1024]{0:T(1024)S(1)} fusion(bf16[1,1024,4096]{2,1,0:T(8,128)(2,1)} %param.9), kind=kLoop, calls=%fused_computation.2 | loop fusion | flops 12581888 | bytes 8392704 | tf_op jit(solution)/shard_map/reduce_sum | solution.py:28
  18.0 52.2 %all-gather.7.cloned.1.call-done = bf16[1,4096,512]{2,1,0:T(8,128)(2,1)} async-done(((bf16[1,256,512]{2,1,0:T(8,128)(2,1)}), bf16[1,4096,512]{2,1,0:T(8,128)(2,1)}) %all-gather.7.cloned.1.call-update) | async-done | bytes 4194320 | tf_op jit(solution)/shard_map/all_gather | solution.py:35
  70.2 0.0 copy-done.2
  70.2 18.1 %fusion.10 = bf16[4096,512]{0,1:T(8,128)(2,1)} fusion(bf16[1,1024,4096]{2,1,0:T(8,128)(2,1)} %param.13, bf16[1,4096,512]{2,1,0:T(8,128)(2,1)} %all-gather.7.cloned.1.call-done, bf16[1,1024,4096]{2,1,0:T(8,128)(2,1)} %param.9, f32[4096]{0:T(1024)S(1)} %copy-done.2, f32[1024]{0:T(1024)S(1)} %add_rsqrt_fusion), kind=kOutput, calls=%fused_computation.11 | convolution fusion | flops 8609333248 | bytes 25186304 | tf_op jit(solution)/shard_map/dot_general | solution.py:47
  88.3 0.0 reduce-scatter.5.cloned.1.call-update
  88.4 0.2 reduce-scatter.3.cloned.1.call-start
  88.6 37.5 %all-gather.5.cloned.1.call-done = bf16[1,4096,512]{2,1,0:T(8,128)(2,1)} async-done(((bf16[1,256,512]{2,1,0:T(8,128)(2,1)}), bf16[1,4096,512]{2,1,0:T(8,128)(2,1)}) %all-gather.5.cloned.1.call-update) | async-done | bytes 4194320 | tf_op jit(solution)/shard_map/all_gather | solution.py:40
  126.1 18.2 %convolution_convert_fusion = bf16[4096,512]{1,0:T(8,128)(2,1)} fusion(bf16[1,1024,4096]{2,1,0:T(8,128)(2,1)} %param.9, f32[4096]{0:T(1024)S(1)} %copy-done.2, f32[1024]{0:T(1024)S(1)} %add_rsqrt_fusion, bf16[1,4096,512]{2,1,0:T(8,128)(2,1)} %all-gather.5.cloned.1.call-done, bf16[1,1024,4096]{2,1,0:T(8,128)(2,1)} %param.13), kind=kOutput, calls=%fused_computation.10 | convolution fusion | flops 8609333248 | bytes 25186304 | tf_op jit(solution)/shard_map/dot_general | solution.py:56
  144.2 0.0 copy-start
  144.2 0.0 copy-start.1
  144.2 0.0 reduce-scatter.3.cloned.1.call-update
  144.3 0.0 all-reduce.2.cloned.1.call-done
  144.3 1.6 copy-done
  145.9 0.3 copy-done.1
  146.2 3.6 %subtract_convert_fusion = (bf16[4096,128]{1,0:T(8,128)(2,1)}, f32[4096,128]{1,0:T(8,128)}) fusion(bf16[4096,128]{1,0:T(8,128)(2,1)} %all-reduce.2.cloned.1.call-done, bf16[4096,128]{1,0:T(8,128)(2,1)S(1)} %copy-done.1, f32[4096,128]{1,0:T(8,128)S(1)} %copy-done), kind=kLoop, calls=%fused_computation.17 | loop fusion | flops 5242880 | bytes 7340032 | tf_op jit(solution)/shard_map/convert_element_type | solution.py:9
  149.9 58.7 %reduce-scatter.5.cloned.1.call-done = bf16[256,512]{0,1:T(8,128)(2,1)} async-done(((bf16[4096,512]{0,1:T(8,128)(2,1)}), bf16[256,512]{0,1:T(8,128)(2,1)}) %reduce-scatter.5.cloned.1.call-update) | async-done | bytes 262160 | tf_op jit(solution)/shard_map/reduce_scatter | solution.py:46
  208.5 1.0 bitcast_convert_fusion
  209.5 1.0 copy.13
  210.5 81.9 %reduce-scatter.3.cloned.1.call-done = bf16[256,512]{1,0:T(8,128)(2,1)} async-done(((bf16[4096,512]{1,0:T(8,128)(2,1)}), bf16[256,512]{1,0:T(8,128)(2,1)}) %reduce-scatter.3.cloned.1.call-update) | async-done | bytes 262160 | tf_op jit(solution)/shard_map/reduce_scatter | solution.py:55
  292.4 1.8 bitcast_convert_fusion.1
  (1 shorter events, 0.0 us)
Async XLA Ops:
  8.0 62.2 %all-gather.7.cloned.1.call-start = ((), (), s32[]{:S(2)}) async-start(), calls=%async_computation.6 | async-start | bytes 4456448 | tf_op jit(solution)/shard_map/all_gather | solution.py:35
  8.7 117.3 %all-gather.5.cloned.1.call-start = ((), (), s32[]{:S(2)}) async-start(), calls=%async_computation.5 | async-start | bytes 4456448 | tf_op jit(solution)/shard_map/all_gather | solution.py:40
  9.5 134.8 %all-reduce.2.cloned.1.call-start = ((), (), s32[]{:S(2)}) async-start(), calls=%async_computation.4 | async-start | bytes 2097152 | tf_op jit(solution)/shard_map/psum | solution.py:67
  12.8 57.4 %copy-start.2 = (f32[4096]{0:T(1024)S(1)}, f32[4096]{0:T(1024)}, u32[]{:S(2)}) copy-start(f32[4096]{0:T(1024)} %param.10) | copy-start | bytes 49156
  12.9 195.7 %reduce-scatter.5.cloned.1.call-start = ((), (), s32[]{:S(2)}) async-start(), calls=%async_computation.3 | async-start | bytes 4456448 | tf_op jit(solution)/shard_map/reduce_scatter | solution.py:46
  88.4 204.0 %reduce-scatter.3.cloned.1.call-start = ((), (), s32[]{:S(2)}) async-start(), calls=%async_computation.2 | async-start | bytes 4456448 | tf_op jit(solution)/shard_map/reduce_scatter | solution.py:55
  144.2 1.7 copy-start
  144.2 2.0 copy-start.1
Sparse Core Ops, SparseCore 0:
  11.3 58.8 all-gather.6
  72.7 53.3 all-gather.4
  130.1 78.4 reduce-scatter.4
  212.9 79.3 reduce-scatter.2
Sparse Core Ops, SparseCore 1:
  13.0 88.8 all-reduce.1
where the time goes:
time: 302 us; the launch traced here: 301 us
  waiting for transfers between devices  232 us (77%)
  matrix products  36.3 us (12%)
  between operations  15.2 us (5%)
  other arithmetic  14.8 us (5%)
    reduce_scatter x1, waiting for transfers between devices, per_device(): lax.psum_scatter(lax.dot_general(normed_cols, value_cot, (((0,), (0,)), (...  81.9 us
    reduce_scatter x1, waiting for transfers between devices, per_device(): lax.psum_scatter(lax.dot_general(cot_cols, values, (((0,), (0,)), ((), ()...  58.7 us
    all_gather x1, waiting for transfers between devices, per_device(): lax.all_gather(value_weight[0], 'fsdp', axis=0, tiled=True)  52.2 us
    all_gather x1, waiting for transfers between devices, per_device(): lax.all_gather(output_weight[0], 'fsdp', axis=0, tiled=True)  37.5 us
    dot_general x1, matrix products, per_device(): lax.dot_general(normed_cols, value_cot, (((0,), (0,)), ((), ())), preferr...  18.2 us
    dot_general x1, matrix products, per_device(): lax.dot_general(cot_cols, values, (((0,), (0,)), ((), ())), preferred_ele...  18.1 us
  transfers between devices with their start and end apart: 5, of which 4 were waited for; matrix products, arithmetic and copies ran while one was open for 17% of the time, Pallas kernels for 0%

commit v1 on v0

v1 whole, which is shorter than its diff:
```python
import functools

import jax
import jax.numpy as jnp
from jax import lax
from jax.experimental import pallas as pl
from jax.experimental.pallas import tpu as pltpu
from jax.sharding import PartitionSpec as P

MESH = pl.DeviceIdType.MESH
F32, BF16 = jnp.float32, jnp.bfloat16
WIDTH, KV, TOK, BLOCK = 4096, 512, 1024, 256
FRAG = 4096
SEG = FRAG // 4
W_CUT = (80, 64, 48, 64)
G_CUT = (144, 144, 112, 112)


def parts(cut):
    a0, a1, b0, b1 = cut
    a, b = a0 + a1, b0 + b1
    return {
        "A0": (0, a0),
        "A1": (a0, a1),
        "A": (0, a),
        "B0": (a, b0),
        "B1": (a + b0, b1),
        "B": (a, b),
        "all": (0, a + b),
    }


W_PART, G_PART = parts(W_CUT), parts(G_CUT)
GATHER_MSGS = 23
REDUCE_MSGS = 23
V_GATHER, O_GATHER = 0, GATHER_MSGS
O_REDUCE, V_REDUCE = 2 * GATHER_MSGS, 2 * GATHER_MSGS + REDUCE_MSGS
DELTA = 2 * GATHER_MSGS + 2 * REDUCE_MSGS
MSGS = DELTA + 7
TOK_PARTS = 8
TOK_ROWS = TOK // TOK_PARTS


def kernel(
    tok_in,
    gain,
    wv_in,
    wo_in,
    cot_in,
    base_in,
    mom_in,
    dv_in,
    exps,
    vg_out,
    og_out,
    nb_out,
    nm_out,
    normed,
    cot,
    wv,
    wo,
    acc,
    factors,
    partial,
    staged,
    from_core,
    from_x,
    from_z,
    base,
    mom,
    scaled,
    segs,
    seg_own,
    seg_x,
    delta,
    grads,
    send_sem,
    recv_sem,
    load_sem,
    store_sem,
):
    r, f = lax.axis_index("replica"), lax.axis_index("fsdp")
    x_lo, y = r // 4, lax.rem(r, 4)
    z, x, c = f // 4, lax.rem(f // 2, 2), lax.rem(f, 2)
    up, down, far = lax.rem(z + 1, 4), lax.rem(z + 3, 4), lax.rem(z + 2, 4)
    other = 1 - x

    def place(zz, xx):
        return {"fsdp": zz * 4 + xx * 2 + c}

    to_core = {"fsdp": z * 4 + x * 2 + (1 - c)}
    to_x, to_up, to_down = place(z, other), place(up, x), place(down, x)
    to_y = [{"replica": x_lo * 4 + lax.rem(y + k, 4)} for k in (1, 2, 3)]
    to_side = {"replica": (1 - x_lo) * 4 + y}

    sent = []

    def send(k, src, dst, to):
        copy = pltpu.make_async_remote_copy(
            src_ref=src,
            dst_ref=dst,
            send_sem=send_sem.at[k],
            recv_sem=recv_sem.at[k],
            device_id=to,
            device_id_type=MESH,
        )
        copy.start()
        sent.append(copy)

    def arrive(k, dst):
        pltpu.make_async_remote_copy(
            src_ref=dst,
            dst_ref=dst,
            send_sem=send_sem.at[k],
            recv_sem=recv_sem.at[k],
            device_id=to_core,
            device_id_type=MESH,
        ).wait_recv()

    loads = {}

    def load(name, src, dst):
        loads[name] = pltpu.make_async_copy(src, dst, load_sem.at[len(loads)])
        loads[name].start()

    def own_rows(buf, zz, xx, cc, part="all"):
        first, count = W_PART[part]
        start = pl.multiple_of(((zz * 2 + xx) * 2 + cc) * BLOCK + first, 16)
        return buf.at[pl.ds(start, count)]

    load("wv", wv_in.at[0], own_rows(wv, z, x, c))
    load("dv", dv_in.at[0], scaled)
    for k in range(TOK_PARTS):
        rows = pl.ds(k * TOK_ROWS, TOK_ROWS)
        load(("tok", k), tok_in.at[0, rows], normed.at[rows])
    load("wo", wo_in.at[0], own_rows(wo, z, x, c))
    load("cot", cot_in.at[0], cot)
    load("base", base_in, base)
    load("mom", mom_in, mom)

    barrier = pltpu.get_barrier_semaphore()
    partners = [to_core, to_x, to_up, to_down, to_side] + to_y
    for to in partners:
        pl.semaphore_signal(barrier, inc=1, device_id=to, device_id_type=MESH)
    pl.semaphore_wait(barrier, len(partners))

    def gather_start(k0, w_in, buf):
        mine = own_rows(buf, z, x, c)
        send(k0 + 0, w_in.at[0], mine, to_x)
        send(k0 + 1, w_in.at[0], mine, to_up)
        send(k0 + 2, w_in.at[0], mine, to_down)
        send(k0 + 3, w_in.at[0], mine, to_core)

    def gather(k0, buf, left, total, factor, own):
        def rows(zz, xx, part="all"):
            return own_rows(buf, zz, xx, c, part)

        def pass_on(k, zz, xx, part, to):
            piece = rows(zz, xx, part)
            send(k0 + k, piece, piece, to)

        def got(k, zz, xx, part="all"):
            arrive(k0 + k, rows(zz, xx, part))

        def multiply(zz, xx, first=False):
            start = pl.multiple_of((zz * 2 + xx) * 2 * BLOCK, 2 * BLOCK)
            both = pl.ds(start, 2 * BLOCK)

            def tile(m, _):
                at = pl.ds(pl.multiple_of(m * 256, 256), 256)
                term = jnp.dot(left[at, both], buf[both, :], preferred_element_type=F32)
                if first:
                    total[at, :] = term
                else:
                    total[at, :] += term
                return 0

            lax.fori_loop(0, TOK // 256, tile, 0)

        def from_sibling(k, zz, xx):
            arrive(k0 + k, own_rows(buf, zz, xx, 1 - c))

        got(0, z, other)
        pass_on(4, z, other, "A", to_up)
        pass_on(5, z, other, "A", to_down)
        pass_on(16, z, other, "all", to_core)
        yield
        got(1, down, x)
        pass_on(6, down, x, "A0", to_up)
        pass_on(7, down, x, "B0", to_up)
        pass_on(8, down, x, "B", to_x)
        pass_on(17, down, x, "all", to_core)
        yield
        got(2, up, x)
        pass_on(9, up, x, "A1", to_down)
        pass_on(10, up, x, "B1", to_down)
        pass_on(11, up, x, "B", to_x)
        pass_on(18, up, x, "all", to_core)
        yield
        loads[own].wait()
        from_sibling(3, z, x)
        multiply(z, x, first=True)
        yield
        from_sibling(16, z, other)
        multiply(z, other)
        yield
        got(4, down, other, "A")
        pass_on(12, down, other, "A0", to_up)
        got(5, up, other, "A")
        pass_on(13, up, other, "A1", to_down)
        yield
        from_sibling(17, down, x)
        multiply(down, x)
        yield
        got(6, far, x, "A0")
        got(7, far, x, "B0")
        pass_on(14, far, x, "B0", to_x)
        got(9, far, x, "A1")
        got(10, far, x, "B1")
        pass_on(15, far, x, "B1", to_x)
        pass_on(21, far, x, "all", to_core)
        yield
        from_sibling(18, up, x)
        multiply(up, x)
        yield
        got(8, down, other, "B")
        pass_on(19, down, other, "all", to_core)
        got(11, up, other, "B")
        pass_on(20, up, other, "all", to_core)
        yield
        from_sibling(21, far, x)
        multiply(far, x)
        yield
        from_sibling(19, down, other)
        multiply(down, other)
        yield
        from_sibling(20, up, other)
        multiply(up, other)
        yield
        got(12, far, other, "A0")
        got(13, far, other, "A1")
        got(14, far, other, "B0")
        got(15, far, other, "B1")
        pass_on(22, far, other, "all", to_core)
        yield
        from_sibling(22, far, other)
        multiply(far, other)

        def turn(m, _):
            at = pl.ds(pl.multiple_of(m * 256, 256), 256)
            factor[:, at] = total[at, :].T.astype(BF16)
            return 0

        lax.fori_loop(0, TOK // 256, turn, 0)
        yield

    dests = [(far, other), (up, other), (down, other), (z, other), (far, x), (up, x), (down, x), (z, x)]

    def reduce(k0, g, factor, right, out, store):
        mine, stage, core_in = partial.at[g], staged.at[g], from_core.at[g]
        x_in, z_in = from_x.at[g], from_z.at[g]

        def cut(ref, part):
            first, count = G_PART[part]
            return ref.at[pl.ds(first, count)]

        def block(d, cc, into):
            zz, xx = dests[d]
            columns = pl.ds(pl.multiple_of(((zz * 2 + xx) * 2 + cc) * BLOCK, BLOCK), BLOCK)

            def tile(m, _):
                at = pl.ds(pl.multiple_of(m * 256, 256), 256)
                term = jnp.dot(factor[at, :], right[:, columns], preferred_element_type=F32)
                into[d, at, :] = term.astype(BF16)
                return 0

            lax.fori_loop(0, KV // 256, tile, 0)

        def compute(d):
            block(d, 1 - c, stage)
            send(k0 + d, stage.at[d], core_in.at[d], to_core)
            block(d, c, mine)

        def add(to, term, count):
            def some(m, _):
                at = pl.ds(pl.multiple_of(m * 16, 16), 16)
                to[at, :] = (to[at, :].astype(F32) + term[at, :].astype(F32)).astype(BF16)
                return 0

            lax.fori_loop(0, count // 16, some, 0, unroll=True)

        def combine(d):
            arrive(k0 + d, core_in.at[d])
            add(mine.at[d], core_in.at[d], KV)

        def add_part(d, part, k, term):
            arrive(k0 + k, term)
            add(cut(mine.at[d], part), term, G_PART[part][1])

        rows_of = {part: G_PART[part][1] for part in G_PART}
        offset = [0]

        def slot(ref, part):
            start = offset[0]
            offset[0] += rows_of[part]
            return ref.at[pl.ds(start, rows_of[part])]

        land = {}
        for k, part in ((8, "B"), (9, "B"), (10, "B"), (11, "B"), (22, "A")):
            land[k] = slot(x_in, part)
        offset[0] = 0
        for k, part in (
            (12, "A0"), (13, "A1"), (14, "A"), (15, "A"), (16, "A0"), (17, "A1"), (18, "B0"), (19, "B1"), (20, "all"), (21, "all"),
        ):
            land[k] = slot(z_in, part)

        def ship(k, d, part, to):
            send(k0 + k, cut(mine.at[d], part), land[k], to)

        compute(0)
        yield
        compute(1)
        combine(0)
        ship(12, 0, "A0", to_up)
        ship(13, 0, "A1", to_down)
        ship(8, 0, "B", to_x)
        yield
        compute(2)
        combine(1)
        ship(9, 1, "B", to_x)
        yield
        compute(3)
        combine(2)
        ship(10, 2, "B", to_x)
        yield
        add_part(1, "A0", 12, land[12])
        ship(14, 1, "A", to_up)
        add_part(2, "A1", 13, land[13])
        ship(15, 2, "A", to_down)
        yield
        compute(4)
        combine(3)
        ship(11, 3, "B", to_x)
        yield
        compute(5)
        combine(4)
        ship(16, 4, "A0", to_up)
        ship(17, 4, "A1", to_down)
        add_part(4, "B", 8, land[8])
        ship(18, 4, "B0", to_up)
        ship(19, 4, "B1", to_down)
        yield
        compute(6)
        combine(5)
        add_part(5, "B", 9, land[9])
        yield
        compute(7)
        combine(6)
        add_part(6, "B", 10, land[10])
        yield
        add_part(5, "A0", 16, land[16])
        add_part(5, "B0", 18, land[18])
        ship(20, 5, "all", to_up)
        add_part(6, "A1", 17, land[17])
        add_part(6, "B1", 19, land[19])
        ship(21, 6, "all", to_down)
        yield
        combine(7)
        add_part(7, "B", 11, land[11])
        yield
        add_part(3, "A", 14, land[14])
        add_part(3, "A", 15, land[15])
        ship(22, 3, "A", to_x)
        yield
        arrive(k0 + 20, land[20])
        arrive(k0 + 21, land[21])
        add(mine.at[7], land[20], KV)
        add(mine.at[7], land[21], KV)
        yield
        add_part(7, "A", 22, land[22])

        def turn(m, _):
            at = pl.ds(pl.multiple_of(m * 128, 128), 128)
            grads[g, :, at] = mine[7, at, :].astype(F32).T
            return 0

        lax.fori_loop(0, KV // 128, turn, 0)
        pltpu.make_async_copy(grads.at[g], out.at[0], store_sem.at[store]).start()
        yield

    def run(task, steps):
        for _ in range(steps):
            next(task, None)

    def finish(task):
        for _ in task:
            pass

    def seg(buf, k):
        return buf.at[pl.ds(pl.multiple_of(lax.rem(y + k, 4) * SEG, SEG), SEG)]

    def outer_step():
        loads["dv"].wait()

        def scale(m, _):
            at = pl.ds(pl.multiple_of(m * 128, 128), 128)
            factor = jnp.exp2(exps[:, at].astype(F32))
            factor = jnp.broadcast_to(factor, (128, 128)).T
            scaled[at, :] = (scaled[at, :].astype(F32) * factor).astype(BF16)
            return 0

        lax.fori_loop(0, FRAG // 128, scale, 0)
        for k in (1, 2, 3):
            send(DELTA + k - 1, seg(scaled, k), segs.at[k - 1], to_y[k - 1])
        yield
        for k in (1, 2, 3):
            arrive(DELTA + k - 1, segs.at[k - 1])
        first = pl.multiple_of(y * SEG, SEG)

        def total(m, _):
            at = pl.ds(pl.multiple_of(m * 32, 32), 32)
            value = scaled[pl.ds(pl.multiple_of(first + m * 32, 32), 32), :].astype(F32)
            for k in range(3):
                value += segs[k, at, :].astype(F32)
            seg_own[at, :] = value.astype(BF16)
            return 0

        lax.fori_loop(0, SEG // 32, total, 0)
        send(DELTA + 3, seg_own, seg_x, to_side)
        yield
        arrive(DELTA + 3, seg_x)

        def both(m, _):
            at = pl.ds(pl.multiple_of(m * 32, 32), 32)
            value = seg_own[at, :].astype(F32) + seg_x[at, :].astype(F32)
            delta[pl.ds(pl.multiple_of(first + m * 32, 32), 32), :] = value.astype(BF16)
            return 0

        lax.fori_loop(0, SEG // 32, both, 0)
        for k in (1, 2, 3):
            send(DELTA + 3 + k, seg(delta, 0), seg(delta, 0), to_y[k - 1])
        yield
        for k in (1, 2, 3):
            arrive(DELTA + 3 + k, seg(delta, 4 - k))
        loads["base"].wait()
        loads["mom"].wait()

        def update(m, _):
            at = pl.ds(pl.multiple_of(m * 64, 64), 64)
            mean = delta[at, :].astype(F32) * 0.125
            new = 0.9 * mom[at, :] + mean
            mom[at, :] = new
            base[at, :] = (base[at, :].astype(F32) - 0.7 * (mean + 0.9 * new)).astype(BF16)
            return 0

        lax.fori_loop(0, FRAG // 64, update, 0)
        pltpu.make_async_copy(base, nb_out, store_sem.at[2]).start()
        pltpu.make_async_copy(mom, nm_out, store_sem.at[3]).start()
        yield

    gather_v = gather(V_GATHER, wv, normed, acc.at[0], factors.at[0], "wv")
    gather_o = gather(O_GATHER, wo, cot, acc.at[1], factors.at[1], "wo")
    reduce_o = reduce(O_REDUCE, 0, factors.at[0], cot, og_out, 0)
    reduce_v = reduce(V_REDUCE, 1, factors.at[1], normed, vg_out, 1)
    outer = outer_step()

    gather_start(V_GATHER, wv_in, wv)
    run(outer, 1)

    for k in range(TOK_PARTS):
        loads[("tok", k)].wait()

        def norm(m, _):
            at = pl.ds(pl.multiple_of(k * TOK_ROWS + m * 16, 16), 16)
            value = normed[at, :].astype(F32)
            scale = lax.rsqrt(jnp.mean(value * value, axis=1, keepdims=True) + 1e-05)
            normed[at, :] = (value * scale * gain[...]).astype(BF16)
            return 0

        lax.fori_loop(0, TOK_ROWS // 16, norm, 0)

    gather_start(O_GATHER, wo_in, wo)
    run(gather_v, 5)
    run(outer, 1)
    loads["cot"].wait()
    run(gather_o, 3)
    run(gather_v, 20)
    for _ in range(6):
        run(gather_o, 2)
        run(reduce_o, 1)
        run(outer, 1)
    run(gather_o, 20)
    run(reduce_o, 3)
    for _ in range(4):
        run(reduce_v, 2)
        run(reduce_o, 1)
    finish(reduce_o)
    finish(reduce_v)
    finish(outer)
    for copy in sent:
        copy.wait_send()
    for src, dst, k in (
        (grads.at[0], og_out.at[0], 0),
        (grads.at[1], vg_out.at[0], 1),
        (base, nb_out, 2),
        (mom, nm_out, 3),
    ):
        pltpu.make_async_copy(src, dst, store_sem.at[k]).wait()


def per_device(tokens, gain, value_w, output_w, cotangent, base, momentum, delta_values, exps):
    any_place, vmem = pl.BlockSpec(memory_space=pl.ANY), pl.BlockSpec(memory_space=pltpu.VMEM)
    grad_x = 4 * G_PART["B"][1] + G_PART["A"][1]
    grad_z = 6 * KV - 3 * G_PART["B"][1]
    return pl.pallas_call(
        kernel,
        out_shape=(
            jax.ShapeDtypeStruct((1, BLOCK, KV), F32),
            jax.ShapeDtypeStruct((1, BLOCK, KV), F32),
            jax.ShapeDtypeStruct((FRAG, 128), BF16),
            jax.ShapeDtypeStruct((FRAG, 128), F32),
        ),
        in_specs=[any_place, vmem, any_place, any_place, any_place, any_place, any_place, any_place, vmem],
        out_specs=(any_place,) * 4,
        scratch_shapes=[
            pltpu.VMEM((TOK, WIDTH), BF16),
            pltpu.VMEM((TOK, WIDTH), BF16),
            pltpu.VMEM((WIDTH, KV), BF16),
            pltpu.VMEM((WIDTH, KV), BF16),
            pltpu.VMEM((2, TOK, KV), F32),
            pltpu.VMEM((2, KV, TOK), BF16),
            pltpu.VMEM((2, 8, KV, BLOCK), BF16),
            pltpu.VMEM((2, 8, KV, BLOCK), BF16),
            pltpu.VMEM((2, 8, KV, BLOCK), BF16),
            pltpu.VMEM((2, grad_x, BLOCK), BF16),
            pltpu.VMEM((2, grad_z, BLOCK), BF16),
            pltpu.VMEM((FRAG, 128), BF16),
            pltpu.VMEM((FRAG, 128), F32),
            pltpu.VMEM((FRAG, 128), BF16),
            pltpu.VMEM((3, SEG, 128), BF16),
            pltpu.VMEM((SEG, 128), BF16),
            pltpu.VMEM((SEG, 128), BF16),
            pltpu.VMEM((FRAG, 128), BF16),
            pltpu.VMEM((2, BLOCK, KV), F32),
            pltpu.SemaphoreType.DMA((MSGS,)),
            pltpu.SemaphoreType.DMA((MSGS,)),
            pltpu.SemaphoreType.DMA((TOK_PARTS + 6,)),
            pltpu.SemaphoreType.DMA((4,)),
        ],
        compiler_params=pltpu.CompilerParams(
            collective_id=0, has_side_effects=True, vmem_limit_bytes=60 * 2**20
        ),
        name="layer_and_outer_step",
    )(tokens, gain.reshape(1, WIDTH), value_w, output_w, cotangent, base, momentum, delta_values, exps)


def solution(mesh):
    return jax.shard_map(
        per_device,
        mesh=mesh,
        in_specs=(
            P("replica", "fsdp", None),
            P(),
            P("replica", "fsdp", None),
            P("replica", "fsdp", None),
            P("replica", "fsdp", None),
            P("fsdp", None),
            P("fsdp", None),
            P("replica", "fsdp", None),
            P("replica", "fsdp"),
        ),
        out_specs=(
            P("replica", "fsdp", None),
            P("replica", "fsdp", None),
            P("fsdp", None),
            P("fsdp", None),
        ),
        check_vma=False,
    )
```

time: 302 us -> 121 us (0.40)
  waiting for transfers between devices: 232 us -> 0 us
  Pallas kernels: 0 us -> 114 us
  matrix products: 36.3 us -> 0 us
  other arithmetic: 14.8 us -> 0 us
  between operations: 15.2 us -> 0.66 us
  local copies, waits for them, and re-layouts: 2.95 us -> 6.18 us
    reduce_scatter x2 -> x0, waiting for transfers between devices: 141 us -> none  [the longest x1 81.9 us: per_device(): lax.psum_scatter(lax.dot_general(normed_cols, value_cot, (((0,), (0,)), (...]
    pallas_call x0 -> x1, Pallas kernels: none -> 114 us  [per_device(): pl.pallas_call(kernel, out_shape=(jax.ShapeDtypeStruct((1, BLOCK, KV), F3...]
    all_gather x2 -> x0, waiting for transfers between devices: 89.7 us -> none  [the longest x1 52.2 us: per_device(): lax.all_gather(value_weight[0], 'fsdp', axis=0, tiled=True)]
    dot_general x2 -> x0, matrix products: 36.3 us -> none  [the longest x1 18.2 us: per_device(): lax.dot_general(normed_cols, value_cot, (((0,), (0,)), ((), ())), preferr...]
    convert_element_type x2 -> x0, other arithmetic: 6.15 us -> none  [the longest x1 3.62 us: nesterov(): (base_part.astype(jnp.float32) - 0.7 * (delta + 0.9 * momentum_next)).ast...]
    reduce_sum x1 -> x0, other arithmetic: 5.07 us -> none  [per_device(): scale = lax.rsqrt(jnp.mean(xf * xf, axis=1, keepdims=True) + 1e-05)]
    unnamed x7 -> x8, local copies, waits for them, and re-layouts: 2.95 us -> 6.18 us
  transfers between devices with their start and end apart: 5 -> 0, of which waited for: 4 -> 0; matrix products, arithmetic and copies ran while one was open for 17% -> 0% of each run, Pallas kernels for 0% -> 0%
where the time goes in v1:
time: 121 us
  Pallas kernels  114 us (94%)
  local copies, waits for them, and re-layouts  6.18 us (5%)
    pallas_call x1, Pallas kernels, per_device(): pl.pallas_call(kernel, out_shape=(jax.ShapeDtypeStruct((1, BLOCK, KV), F3...  114 us
    unnamed x8, local copies, waits for them, and re-layouts  6.18 us

profile of v1, /device:TPU:0, one launch (start us, length us, event | category | flops | bytes accessed | tf_op | source)
XLA Modules:
  0.0 121.1 jit_solution(511913702912131160)
XLA Ops:
  0.6 114.2 %layer_and_outer_step.1 = (f32[1,256,512]{2,1,0:T(8,128)}, f32[1,256,512]{2,1,0:T(8,128)}, bf16[4096,128]{1,0:T(8,128)(2,1)}, f32[4096,128]{1,0:T(8,128)}) custom-call(bf16[1,1024,4096]{2,1,0:T(8,128)(2,1)} %tok_in.1, f32[1,4096]{1,0:T(1,128)} %bitcast.1, bf16[1,256,512]{2,1,0:T(8,128)(2,1)} %wv_in.1, bf16[1,256,512]{2,1,0:T(8,128)(2,1)} %wo_in.1, ...), custom_call_target="tpu_custom_call" | custom-call | tf_op jit(solution)/shard_map/layer_and_outer_step/pallas_call | solution.py:515
  114.9 0.0 copy-start.1
  114.9 0.0 copy-start
  114.9 2.0 %copy.17 = f32[1,256,512]{2,1,0:T(8,128)} copy(f32[1,256,512]{2,1,0:T(8,128)} %get-tuple-element.8) | data formatting | bytes 1048576
  116.9 1.9 %copy.18 = f32[1,256,512]{2,1,0:T(8,128)} copy(f32[1,256,512]{2,1,0:T(8,128)} %get-tuple-element.9) | data formatting | bytes 1048576
  118.8 0.0 copy-done.1
  118.8 1.0 copy.19
  119.7 0.0 copy-done
  119.7 1.3 %copy.20 = f32[4096,128]{1,0:T(8,128)} copy(f32[4096,128]{1,0:T(8,128)S(1)} %copy-done) | data formatting | bytes 4194304
Async XLA Ops:
  114.9 3.9 %copy-start.1 = (bf16[4096,128]{1,0:T(8,128)(2,1)S(1)}, bf16[4096,128]{1,0:T(8,128)(2,1)}, u32[]{:S(2)}) copy-start(bf16[4096,128]{1,0:T(8,128)(2,1)} %get-tuple-element.10) | copy-start | bytes 3145732
  114.9 4.9 %copy-start = (f32[4096,128]{1,0:T(8,128)S(1)}, f32[4096,128]{1,0:T(8,128)}, u32[]{:S(2)}) copy-start(f32[4096,128]{1,0:T(8,128)} %get-tuple-element.11) | copy-start | bytes 6291460

commit v2 on v0

v2 whole, which is shorter than its diff:
```python
import jax
import jax.numpy as jnp
from jax import lax
from jax.experimental import pallas as pl
from jax.experimental.pallas import tpu as pltpu
from jax.sharding import PartitionSpec as P

MESH = pl.DeviceIdType.MESH
F32, BF16 = jnp.float32, jnp.bfloat16
WIDTH, KV, TOK, BLOCK = 4096, 512, 1024, 256
FRAG = 4096
SEG = FRAG // 4
NORM_ROWS = 64
TOK_PARTS = 8
UPDATES = 4

CUTS = ({"A0": 80, "A1": 80, "B0": 48, "B1": 48},) * 2


def plan():
    found = []

    def send(link, block, part, cause):
        dz, dx = block
        lands = {"U": ((dz + 3) % 4, dx), "D": ((dz + 1) % 4, dx), "S": (dz, 1 - dx)}[link]
        found.append((link, block, lands, part, cause))

    for part in ("A0", "A1", "B0", "B1"):
        send("S", (0, 0), part, None)
    for part in ("A0", "B0", "B1", "A1"):
        send("U", (0, 0), part, None)
    for part in ("A1", "B1", "B0", "A0"):
        send("D", (0, 0), part, None)
    k = 0
    while k < len(found):
        link, _, at, part, _ = found[k]
        if at == (0, 1) and part in ("A0", "A1"):
            send("U", at, part, k)
            send("D", at, part, k)
        if at in ((3, 0), (3, 1)) and link == "U" and part in ("A0", "B0"):
            send("U", at, part, k)
        if at in ((1, 0), (1, 1)) and link == "D" and part in ("A1", "B1"):
            send("D", at, part, k)
        if at[1] == 0 and link != "S" and part in ("B0", "B1"):
            send("S", at, part, k)
        k += 1
    return found


PLAN = plan()
CHILDREN = [[c for c, m in enumerate(PLAN) if m[4] == k] for k in range(len(PLAN))]
BLOCKS = [(dz, dx) for dx in (1, 0) for dz in (2, 1, 3, 0)]
COUNT = len(PLAN)
GROUP = COUNT + len(BLOCKS)
DELTA = 4 * GROUP
MSGS = DELTA + 7
BACK = {"U": "D", "D": "U", "S": "S"}
ORDER = (
    ("start", 0, 0), ("scale", 0, 0), ("mul", 0, 7), ("norm", 0, 0), ("norm", 0, 1), ("rx", 0, 4), ("rx", 0, 8),
    ("norm", 0, 2), ("norm", 0, 3), ("rx", 0, 0), ("norm", 0, 4), ("rx", 0, 5), ("rx", 0, 9), ("norm", 0, 5),
    ("norm", 0, 6), ("norm", 0, 7), ("rx", 0, 6), ("rx", 0, 10), ("rx", 0, 1), ("start", 1, 0), ("norm", 0, 8),
    ("norm", 0, 9), ("rx", 0, 2), ("norm", 0, 10), ("rx", 0, 7), ("rx", 0, 11), ("norm", 0, 11), ("norm", 0, 12),
    ("rx", 0, 3), ("norm", 0, 13), ("norm", 0, 14), ("norm", 0, 15), ("rx", 0, 18), ("rx", 0, 16), ("rx", 0, 20),
    ("mul", 1, 7), ("mul", 0, 6), ("rx", 0, 22), ("mul", 0, 5), ("rx", 0, 12), ("rx", 0, 13), ("rx", 0, 19),
    ("mul", 0, 3), ("rx", 0, 17), ("rx", 0, 21), ("rx", 0, 23), ("rx", 0, 14), ("rx", 0, 15), ("rx", 1, 0),
    ("dsum", 0, 0), ("mul", 0, 4), ("rx", 1, 4), ("rx", 1, 8), ("rx", 1, 1), ("mul", 0, 2), ("rx", 1, 5), ("rx", 1, 9),
    ("rx", 1, 2), ("mul", 0, 1), ("rx", 1, 6), ("rx", 1, 10), ("rx", 1, 3), ("rx", 0, 26), ("rx", 1, 7), ("rx", 1, 11),
    ("rx", 0, 27), ("mul", 1, 3), ("rx", 0, 24), ("rx", 0, 25), ("mul", 1, 6), ("mul", 1, 5), ("rx", 1, 12),
    ("rx", 1, 13), ("mul", 0, 0), ("blk", 0, 0), ("rx", 1, 16), ("rx", 1, 20), ("blk", 0, 1), ("dboth", 0, 0),
    ("blk", 0, 2), ("rx", 1, 15), ("rx", 1, 14), ("rx", 1, 18), ("blk", 0, 3), ("rx", 1, 17), ("rx", 1, 21),
    ("rx", 1, 22), ("cmb", 0, 0), ("cmb", 0, 1), ("blk", 0, 4), ("rx", 1, 19), ("rx", 1, 24), ("cmb", 0, 2),
    ("rx", 1, 23), ("blk", 0, 5), ("cmb", 0, 3), ("rx", 1, 25), ("blk", 0, 6), ("rx", 1, 26), ("cmb", 0, 4),
    ("blk", 0, 7), ("rx", 1, 27), ("snd", 0, 15), ("snd", 0, 12), ("mul", 1, 4), ("snd", 0, 17), ("cmb", 0, 5),
    ("mul", 1, 2), ("snd", 0, 21), ("cmb", 0, 6), ("mul", 1, 1), ("cmb", 0, 7), ("snd", 0, 4), ("snd", 0, 8),
    ("mul", 1, 0), ("snd", 0, 10), ("blk", 1, 0), ("snd", 0, 0), ("snd", 0, 1), ("blk", 1, 1), ("snd", 0, 5),
    ("snd", 0, 6), ("blk", 1, 2), ("blk", 1, 3), ("snd", 0, 9), ("cmb", 1, 0), ("cmb", 1, 1), ("blk", 1, 4),
    ("cmb", 1, 2), ("blk", 1, 5), ("cmb", 1, 3), ("blk", 1, 6), ("blk", 1, 7), ("cmb", 1, 4), ("snd", 1, 17),
    ("snd", 1, 12), ("snd", 1, 15), ("cmb", 1, 5), ("snd", 1, 21), ("fin", 0, 0), ("fin", 0, 2), ("fin", 0, 3),
    ("fin", 0, 1), ("cmb", 1, 6), ("upd", 0, 0), ("cmb", 1, 7), ("upd", 0, 1), ("snd", 1, 10), ("upd", 0, 2),
    ("upd", 0, 3), ("snd", 1, 4), ("snd", 1, 8), ("snd", 1, 6), ("snd", 1, 5), ("snd", 1, 1), ("snd", 1, 0),
    ("snd", 1, 9), ("fin", 1, 1), ("fin", 1, 2), ("fin", 1, 3), ("fin", 1, 0),
)


def kernel(
    tok_in,
    gain,
    wv_in,
    wo_in,
    cot_in,
    base_in,
    mom_in,
    dv_in,
    exps,
    vg_out,
    og_out,
    base,
    mom,
    normed,
    cot,
    wv,
    wo,
    acc,
    factors,
    partial,
    from_core,
    landed,
    scaled,
    segs,
    seg_own,
    seg_x,
    delta,
    send_sem,
    recv_sem,
    load_sem,
):
    r, f = lax.axis_index("replica"), lax.axis_index("fsdp")
    x_lo, y = r // 4, lax.rem(r, 4)
    z, x, c = f // 4, lax.rem(f // 2, 2), lax.rem(f, 2)

    def chip(block):
        dz, dx = block
        return lax.rem(z + dz, 4) * 2 + (1 - x if dx else x)

    to_core = {"fsdp": chip((0, 0)) * 2 + 1 - c}
    to = {"U": {"fsdp": chip((1, 0)) * 2 + c}, "D": {"fsdp": chip((3, 0)) * 2 + c}, "S": {"fsdp": chip((0, 1)) * 2 + c}}
    to_y = [{"replica": x_lo * 4 + lax.rem(y + k, 4)} for k in (1, 2, 3)]
    to_side = {"replica": (1 - x_lo) * 4 + y}

    sent = []

    def copy_of(k, src, dst, device):
        return pltpu.make_async_remote_copy(
            src_ref=src,
            dst_ref=dst,
            send_sem=send_sem.at[k],
            recv_sem=recv_sem.at[k],
            device_id=device,
            device_id_type=MESH,
        )

    def send(k, src, dst, device):
        sent.append(copy_of(k, src, dst, device))
        sent[-1].start()

    def arrive(k, dst):
        copy_of(k, dst, dst, to_core).wait_recv()

    loads, waited = {}, set()

    def load(name, src, dst):
        loads[name] = pltpu.make_async_copy(src, dst, load_sem.at[len(loads)])
        loads[name].start()

    def loaded(name):
        if name not in waited:
            waited.add(name)
            loads[name].wait()

    weights, weights_in = (wo, wv), (wo_in, wv_in)
    left, right, outs = (cot, normed), (normed, cot), (vg_out, og_out)

    def rows_of(g, part):
        cut = CUTS[g]
        first = 0
        for name in ("A0", "A1", "B0", "B1"):
            if name == part:
                return first, cut[name]
            first += cut[name]
        return 0, BLOCK

    def weight(g, block, core, part=None):
        first, count = rows_of(g, part)
        return weights[g].at[pl.ds(pl.multiple_of((chip(block) * 2 + core) * BLOCK + first, 16), count)]

    barrier = pltpu.get_barrier_semaphore()
    partners = [to_core, to["U"], to["D"], to["S"], to_side] + to_y
    for device in partners:
        pl.semaphore_signal(barrier, inc=1, device_id=device, device_id_type=MESH)
    pl.semaphore_wait(barrier, len(partners))

    load("own0", wo_in.at[0], weight(0, (0, 0), c))
    load("own1", wv_in.at[0], weight(1, (0, 0), c))

    def load_rest():
        load("dv", dv_in.at[0], scaled)
        load("cot", cot_in.at[0], cot)
        for k in range(TOK_PARTS):
            rows = pl.ds(k * (TOK // TOK_PARTS), TOK // TOK_PARTS)
            load(("tok", k), tok_in.at[0, rows], normed.at[rows])
        load("base", base_in, base)
        load("mom", mom_in, mom)

    received = {}
    multiplied = [0, 0]

    def start(g, _):
        own = {link: [k for k, m in enumerate(PLAN) if m[4] is None and m[0] == link] for link in "SUD"}
        for i in range(4):
            for link in "SUD":
                k = own[link][i]
                first, count = rows_of(g, PLAN[k][3])
                piece = weights_in[g].at[0, pl.ds(first, count)]
                send(g * GROUP + k, piece, weight(g, (0, 0), c, PLAN[k][3]), to[link])
        send(g * GROUP + COUNT + BLOCKS.index((0, 0)), weights_in[g].at[0], weight(g, (0, 0), c), to_core)

    def rx(g, k):
        _, _, block, part, _ = PLAN[k]
        piece = weight(g, block, c, part)
        arrive(g * GROUP + k, piece)
        for child in CHILDREN[k]:
            send(g * GROUP + child, piece, piece, to[PLAN[child][0]])
        received[g, block] = received.get((g, block), 0) + 1
        if received[g, block] == 4:
            whole = weight(g, block, c)
            send(g * GROUP + COUNT + BLOCKS.index(block), whole, whole, to_core)

    def mul(g, b):
        block = BLOCKS[b]
        if block == (0, 0):
            loaded("own%d" % g)
        if g == 0:
            loaded("cot")
        arrive(g * GROUP + COUNT + b, weight(g, block, 1 - c))
        both = pl.ds(pl.multiple_of(chip(block) * 2 * BLOCK, 2 * BLOCK), 2 * BLOCK)
        term = jnp.dot(left[g][:, both], weights[g][both, :], preferred_element_type=F32)
        multiplied[g] += 1
        if multiplied[g] == 1:
            acc[g] = term
        elif multiplied[g] < len(BLOCKS):
            acc[g] += term
        else:
            factors[g] = (acc[g] + term).astype(BF16)

    def mine(g, b, part=None):
        first, count = rows_of(g, part)
        return partial.at[g, b, pl.ds(pl.multiple_of(c * BLOCK + first, 16), count)]

    def slot(g, k):
        first = sum(CUTS[g][m[3]] for m in PLAN[:k])
        return landed.at[g, pl.ds(first, CUTS[g][PLAN[k][3]])]

    def add(ref, term):
        ref[...] = (ref[...].astype(F32) + term[...].astype(F32)).astype(BF16)

    def blk(g, b):
        columns = pl.ds(pl.multiple_of(chip(BLOCKS[b]) * 2 * BLOCK, 2 * BLOCK), 2 * BLOCK)
        term = lax.dot_general(right[g][:, columns], factors[g], (((0,), (0,)), ((), ())), preferred_element_type=F32)
        partial[g, b] = term.astype(BF16)
        theirs = partial.at[g, b, pl.ds(pl.multiple_of((1 - c) * BLOCK, BLOCK), BLOCK)]
        send((2 + g) * GROUP + COUNT + b, theirs, from_core.at[g, b], to_core)

    def ship(g, k):
        link, _, block, part, _ = PLAN[k]
        send((2 + g) * GROUP + k, mine(g, BLOCKS.index(block), part), slot(g, k), to[BACK[link]])

    def cmb(g, b):
        arrive((2 + g) * GROUP + COUNT + b, from_core.at[g, b])
        add(mine(g, b), from_core.at[g, b])
        for k, m in enumerate(PLAN):
            if m[2] == BLOCKS[b] and not CHILDREN[k]:
                ship(g, k)

    def snd(g, k):
        piece = mine(g, BLOCKS.index(PLAN[k][2]), PLAN[k][3])
        for child in CHILDREN[k]:
            arrive((2 + g) * GROUP + child, slot(g, child))
            add(piece, slot(g, child))
        ship(g, k)

    def fin(g, i):
        part = ("A0", "A1", "B0", "B1")[i]
        first, count = rows_of(g, part)
        total = mine(g, BLOCKS.index((0, 0)), part)[...].astype(F32)
        for k, m in enumerate(PLAN):
            if m[4] is None and m[3] == part:
                arrive((2 + g) * GROUP + k, slot(g, k))
                total += slot(g, k)[...].astype(F32)
        outs[g][0, pl.ds(first, count), :] = total

    def norm(_, i):
        loaded(("tok", i * NORM_ROWS // (TOK // TOK_PARTS)))
        at = pl.ds(i * NORM_ROWS, NORM_ROWS)
        value = normed[at, :].astype(F32)
        scale = lax.rsqrt(jnp.mean(value * value, axis=1, keepdims=True) + 1e-05)
        normed[at, :] = (value * scale * gain[...]).astype(BF16)

    def seg(buf, k):
        return buf.at[pl.ds(pl.multiple_of(lax.rem(y + k, 4) * SEG, SEG), SEG)]

    def scale(_, __):
        loaded("dv")

        def some(m, _):
            at = pl.ds(pl.multiple_of(m * 128, 128), 128)
            factor = jnp.exp2(exps[:, at].astype(F32))
            factor = jnp.broadcast_to(factor, (128, 128)).T
            scaled[at, :] = (scaled[at, :].astype(F32) * factor).astype(BF16)
            return 0

        lax.fori_loop(0, FRAG // 128, some, 0, unroll=4)
        for k in (1, 2, 3):
            send(DELTA + k - 1, seg(scaled, k), segs.at[k - 1], to_y[k - 1])

    def dsum(_, __):
        for k in (1, 2, 3):
            arrive(DELTA + k - 1, segs.at[k - 1])

        def some(m, _):
            at = pl.ds(pl.multiple_of(m * 128, 128), 128)
            value = scaled[pl.ds(pl.multiple_of(y * SEG + m * 128, 128), 128), :].astype(F32)
            for k in range(3):
                value += segs[k, at, :].astype(F32)
            seg_own[at, :] = value.astype(BF16)
            return 0

        lax.fori_loop(0, SEG // 128, some, 0)
        send(DELTA + 3, seg_own, seg_x, to_side)

    def dboth(_, __):
        arrive(DELTA + 3, seg_x)

        def some(m, _):
            at = pl.ds(pl.multiple_of(m * 128, 128), 128)
            value = seg_own[at, :].astype(F32) + seg_x[at, :].astype(F32)
            delta[pl.ds(pl.multiple_of(y * SEG + m * 128, 128), 128), :] = value.astype(BF16)
            return 0

        lax.fori_loop(0, SEG // 128, some, 0)
        for k in (1, 2, 3):
            send(DELTA + 3 + k, seg(delta, 0), seg(delta, 0), to_y[k - 1])

    def upd(_, i):
        if i == 0:
            for k in (1, 2, 3):
                arrive(DELTA + 3 + k, seg(delta, 4 - k))
            loaded("base")
            loaded("mom")

        def some(m, _):
            at = pl.ds(pl.multiple_of(i * (FRAG // UPDATES) + m * 128, 128), 128)
            mean = delta[at, :].astype(F32) * 0.125
            new = 0.9 * mom[at, :] + mean
            mom[at, :] = new
            base[at, :] = (base[at, :].astype(F32) - 0.7 * (mean + 0.9 * new)).astype(BF16)
            return 0

        lax.fori_loop(0, FRAG // UPDATES // 128, some, 0)

    tasks = {
        "start": start,
        "rx": rx,
        "mul": mul,
        "blk": blk,
        "cmb": cmb,
        "snd": snd,
        "fin": fin,
        "norm": norm,
        "scale": scale,
        "dsum": dsum,
        "dboth": dboth,
        "upd": upd,
    }
    for name, g, k in ORDER:
        tasks[name](g, k)
        if (name, g) == ("start", 0):
            load_rest()
    for copy in sent:
        copy.wait_send()


def hand_over(*refs):
    sem = refs[-1]
    arrays = (len(refs) - 1) // 2
    copies = [pltpu.make_async_copy(refs[k], refs[arrays + k], sem.at[k]) for k in range(arrays)]
    for copy in copies:
        copy.start()
    for copy in copies:
        copy.wait()


def per_device(tokens, gain, value_w, output_w, cotangent, base, momentum, delta_values, exps):
    any_place, vmem = pl.BlockSpec(memory_space=pl.ANY), pl.BlockSpec(memory_space=pltpu.VMEM)
    landing = max(sum(cut[m[3]] for m in PLAN) for cut in CUTS)
    shapes = (((1, BLOCK, KV), F32), ((1, BLOCK, KV), F32), ((FRAG, 128), BF16), ((FRAG, 128), F32))
    results = pl.pallas_call(
        kernel,
        out_shape=tuple(pltpu.VMEM(*shape) for shape in shapes),
        in_specs=[any_place, vmem, any_place, any_place, any_place, any_place, any_place, any_place, vmem],
        out_specs=(vmem,) * 4,
        scratch_shapes=[
            pltpu.VMEM((TOK, WIDTH), BF16),
            pltpu.VMEM((TOK, WIDTH), BF16),
            pltpu.VMEM((WIDTH, KV), BF16),
            pltpu.VMEM((WIDTH, KV), BF16),
            pltpu.VMEM((2, TOK, KV), F32),
            pltpu.VMEM((2, TOK, KV), BF16),
            pltpu.VMEM((2, 8, 2 * BLOCK, KV), BF16),
            pltpu.VMEM((2, 8, BLOCK, KV), BF16),
            pltpu.VMEM((2, landing, KV), BF16),
            pltpu.VMEM((FRAG, 128), BF16),
            pltpu.VMEM((3, SEG, 128), BF16),
            pltpu.VMEM((SEG, 128), BF16),
            pltpu.VMEM((SEG, 128), BF16),
            pltpu.VMEM((FRAG, 128), BF16),
            pltpu.SemaphoreType.DMA((MSGS,)),
            pltpu.SemaphoreType.DMA((MSGS,)),
            pltpu.SemaphoreType.DMA((TOK_PARTS + 6,)),
        ],
        compiler_params=pltpu.CompilerParams(
            collective_id=0, has_side_effects=True, vmem_limit_bytes=54 * 2**20
        ),
        name="layer_and_outer_step",
    )(tokens, gain.reshape(1, WIDTH), value_w, output_w, cotangent, base, momentum, delta_values, exps)
    return pl.pallas_call(
        hand_over,
        out_shape=tuple(jax.ShapeDtypeStruct(*shape) for shape in shapes),
        in_specs=[vmem] * 4,
        out_specs=(any_place,) * 4,
        scratch_shapes=[pltpu.SemaphoreType.DMA((4,))],
        compiler_params=pltpu.CompilerParams(vmem_limit_bytes=2**20),
        name="hand_over",
    )(*(pltpu.with_memory_space_constraint(result, pltpu.VMEM) for result in results))


def solution(mesh):
    return jax.shard_map(
        per_device,
        mesh=mesh,
        in_specs=(
            P("replica", "fsdp", None),
            P(),
            P("replica", "fsdp", None),
            P("replica", "fsdp", None),
            P("replica", "fsdp", None),
            P("fsdp", None),
            P("fsdp", None),
            P("replica", "fsdp", None),
            P("replica", "fsdp"),
        ),
        out_specs=(
            P("replica", "fsdp", None),
            P("replica", "fsdp", None),
            P("fsdp", None),
            P("fsdp", None),
        ),
        check_vma=False,
    )
```

time: 302 us -> 72.3 us (0.24)
  waiting for transfers between devices: 232 us -> 0 us
  Pallas kernels: 0 us -> 70.8 us
  matrix products: 36.3 us -> 0 us
  other arithmetic: 14.8 us -> 0 us
  between operations: 15.2 us -> 0.8 us
    reduce_scatter x2 -> x0, waiting for transfers between devices: 141 us -> none  [the longest x1 81.9 us: per_device(): lax.psum_scatter(lax.dot_general(normed_cols, value_cot, (((0,), (0,)), (...]
    all_gather x2 -> x0, waiting for transfers between devices: 89.7 us -> none  [the longest x1 52.2 us: per_device(): lax.all_gather(value_weight[0], 'fsdp', axis=0, tiled=True)]
    pallas_call x0 -> x2, Pallas kernels: none -> 70.8 us  [the longest x1 68.8 us: per_device(): pl.pallas_call(kernel, out_shape=tuple((pltpu.VMEM(*shape) for shape in s...]
    dot_general x2 -> x0, matrix products: 36.3 us -> none  [the longest x1 18.2 us: per_device(): lax.dot_general(normed_cols, value_cot, (((0,), (0,)), ((), ())), preferr...]
    convert_element_type x2 -> x0, other arithmetic: 6.15 us -> none  [the longest x1 3.62 us: nesterov(): (base_part.astype(jnp.float32) - 0.7 * (delta + 0.9 * momentum_next)).ast...]
    reduce_sum x1 -> x0, other arithmetic: 5.07 us -> none  [per_device(): scale = lax.rsqrt(jnp.mean(xf * xf, axis=1, keepdims=True) + 1e-05)]
  transfers between devices with their start and end apart: 5 -> 0, of which waited for: 4 -> 0; matrix products, arithmetic and copies ran while one was open for 17% -> 0% of each run, Pallas kernels for 0% -> 0%
where the time goes in v2:
time: 72.3 us; the launch traced here: 71.6 us
  Pallas kernels  70.8 us (98%)
  between operations  0.8 us (1%)
    pallas_call x1, Pallas kernels, per_device(): pl.pallas_call(kernel, out_shape=tuple((pltpu.VMEM(*shape) for shape in s...  68.8 us
    pallas_call x1, Pallas kernels, per_device(): pl.pallas_call(hand_over, out_shape=tuple((jax.ShapeDtypeStruct(*shape) f...  2.05 us

profile of v2, /device:TPU:0, one launch (start us, length us, event | category | flops | bytes accessed | tf_op | source)
XLA Modules:
  0.0 71.6 jit_solution(10798254339171343036)
XLA Ops:
  0.6 68.8 %layer_and_outer_step.1 = (f32[1,256,512]{2,1,0:T(8,128)S(1)}, f32[1,256,512]{2,1,0:T(8,128)S(1)}, bf16[4096,128]{1,0:T(8,128)(2,1)S(1)}, f32[4096,128]{1,0:T(8,128)S(1)}) custom-call(bf16[1,1024,4096]{2,1,0:T(8,128)(2,1)} %tok_in.1, f32[1,4096]{1,0:T(1,128)} %bitcast.1, bf16[1,256,512]{2,1,0:T(8,128)(2,1)} %wv_in.1, bf16[1,256,512]{2,1,0:T(8,128)(2,1)} %wo_in.1, ...), custom_call_target="tpu_custom_call" | custom-call | tf_op jit(solution)/shard_map/layer_and_outer_step/pallas_call | solution.py:386
  69.4 2.0 %hand_over.1 = (f32[1,256,512]{2,1,0:T(8,128)}, f32[1,256,512]{2,1,0:T(8,128)}, bf16[4096,128]{1,0:T(8,128)(2,1)}, f32[4096,128]{1,0:T(8,128)}) custom-call(f32[1,256,512]{2,1,0:T(8,128)S(1)} %get-tuple-element.8.refs_0_, f32[1,256,512]{2,1,0:T(8,128)S(1)} %get-tuple-element.9.refs_1_, bf16[4096,128]{1,0:T(8,128)(2,1)S(1)} %get-tuple-element.10.refs_2_, ...), custom_call_target="tpu_custom_call" | custom-call | tf_op jit(solution)/shard_map/hand_over/pallas_call | solution.py:415

commit v3 on v2

--- a/solution.py
+++ b/solution.py
@@ -56,29 +56,33 @@
 MSGS = DELTA + 7
 BACK = {"U": "D", "D": "U", "S": "S"}
 ORDER = (
-    ("start", 0, 0), ("scale", 0, 0), ("mul", 0, 7), ("norm", 0, 0), ("norm", 0, 1), ("rx", 0, 4), ("rx", 0, 8),
-    ("norm", 0, 2), ("norm", 0, 3), ("rx", 0, 0), ("norm", 0, 4), ("rx", 0, 5), ("rx", 0, 9), ("norm", 0, 5),
-    ("norm", 0, 6), ("norm", 0, 7), ("rx", 0, 6), ("rx", 0, 10), ("rx", 0, 1), ("start", 1, 0), ("norm", 0, 8),
-    ("norm", 0, 9), ("rx", 0, 2), ("norm", 0, 10), ("rx", 0, 7), ("rx", 0, 11), ("norm", 0, 11), ("norm", 0, 12),
-    ("rx", 0, 3), ("norm", 0, 13), ("norm", 0, 14), ("norm", 0, 15), ("rx", 0, 18), ("rx", 0, 16), ("rx", 0, 20),
-    ("mul", 1, 7), ("mul", 0, 6), ("rx", 0, 22), ("mul", 0, 5), ("rx", 0, 12), ("rx", 0, 13), ("rx", 0, 19),
-    ("mul", 0, 3), ("rx", 0, 17), ("rx", 0, 21), ("rx", 0, 23), ("rx", 0, 14), ("rx", 0, 15), ("rx", 1, 0),
-    ("dsum", 0, 0), ("mul", 0, 4), ("rx", 1, 4), ("rx", 1, 8), ("rx", 1, 1), ("mul", 0, 2), ("rx", 1, 5), ("rx", 1, 9),
-    ("rx", 1, 2), ("mul", 0, 1), ("rx", 1, 6), ("rx", 1, 10), ("rx", 1, 3), ("rx", 0, 26), ("rx", 1, 7), ("rx", 1, 11),
-    ("rx", 0, 27), ("mul", 1, 3), ("rx", 0, 24), ("rx", 0, 25), ("mul", 1, 6), ("mul", 1, 5), ("rx", 1, 12),
-    ("rx", 1, 13), ("mul", 0, 0), ("blk", 0, 0), ("rx", 1, 16), ("rx", 1, 20), ("blk", 0, 1), ("dboth", 0, 0),
-    ("blk", 0, 2), ("rx", 1, 15), ("rx", 1, 14), ("rx", 1, 18), ("blk", 0, 3), ("rx", 1, 17), ("rx", 1, 21),
-    ("rx", 1, 22), ("cmb", 0, 0), ("cmb", 0, 1), ("blk", 0, 4), ("rx", 1, 19), ("rx", 1, 24), ("cmb", 0, 2),
-    ("rx", 1, 23), ("blk", 0, 5), ("cmb", 0, 3), ("rx", 1, 25), ("blk", 0, 6), ("rx", 1, 26), ("cmb", 0, 4),
-    ("blk", 0, 7), ("rx", 1, 27), ("snd", 0, 15), ("snd", 0, 12), ("mul", 1, 4), ("snd", 0, 17), ("cmb", 0, 5),
-    ("mul", 1, 2), ("snd", 0, 21), ("cmb", 0, 6), ("mul", 1, 1), ("cmb", 0, 7), ("snd", 0, 4), ("snd", 0, 8),
-    ("mul", 1, 0), ("snd", 0, 10), ("blk", 1, 0), ("snd", 0, 0), ("snd", 0, 1), ("blk", 1, 1), ("snd", 0, 5),
-    ("snd", 0, 6), ("blk", 1, 2), ("blk", 1, 3), ("snd", 0, 9), ("cmb", 1, 0), ("cmb", 1, 1), ("blk", 1, 4),
-    ("cmb", 1, 2), ("blk", 1, 5), ("cmb", 1, 3), ("blk", 1, 6), ("blk", 1, 7), ("cmb", 1, 4), ("snd", 1, 17),
-    ("snd", 1, 12), ("snd", 1, 15), ("cmb", 1, 5), ("snd", 1, 21), ("fin", 0, 0), ("fin", 0, 2), ("fin", 0, 3),
-    ("fin", 0, 1), ("cmb", 1, 6), ("upd", 0, 0), ("cmb", 1, 7), ("upd", 0, 1), ("snd", 1, 10), ("upd", 0, 2),
-    ("upd", 0, 3), ("snd", 1, 4), ("snd", 1, 8), ("snd", 1, 6), ("snd", 1, 5), ("snd", 1, 1), ("snd", 1, 0),
-    ("snd", 1, 9), ("fin", 1, 1), ("fin", 1, 2), ("fin", 1, 3), ("fin", 1, 0),
+    ("own", 0, 0), ("own", 0, 4), ("own", 0, 8), ("own", 0, 1), ("own", 0, 5), ("own", 0, 9), ("own", 0, 2),
+    ("own", 0, 6), ("own", 0, 10), ("own", 0, 3), ("own", 0, 7), ("own", 0, 11), ("load", 0, 0), ("start", 0, 0),
+    ("scale", 0, 0), ("dsend", 0, 0), ("rx", 0, 8), ("norm", 0, 0), ("rx", 0, 5), ("rx", 0, 0), ("rx", 0, 9),
+    ("norm", 0, 1), ("rx", 0, 4), ("norm", 0, 2), ("rx", 0, 10), ("rx", 0, 6), ("rx", 0, 1), ("mul", 0, 7),
+    ("own", 1, 8), ("own", 1, 9), ("rx", 0, 11), ("own", 1, 4), ("norm", 0, 3), ("rx", 0, 17), ("norm", 0, 4),
+    ("rx", 0, 2), ("norm", 0, 5), ("norm", 0, 6), ("own", 1, 0), ("rx", 0, 3), ("norm", 0, 7), ("norm", 0, 8),
+    ("norm", 0, 9), ("mul", 0, 5), ("rx", 0, 22), ("own", 1, 5), ("own", 1, 6), ("rx", 0, 21), ("rx", 0, 18),
+    ("rx", 0, 20), ("rx", 0, 16), ("rx", 0, 19), ("rx", 0, 23), ("own", 1, 10), ("own", 1, 1), ("own", 1, 2),
+    ("rx", 0, 7), ("own", 1, 3), ("norm", 0, 10), ("rx", 0, 26), ("rx", 0, 13), ("norm", 0, 11), ("rx", 0, 15),
+    ("norm", 0, 12), ("rx", 0, 12), ("rx", 0, 14), ("own", 1, 11), ("mul", 0, 3), ("own", 1, 7), ("norm", 0, 13),
+    ("mul", 0, 4), ("start", 1, 0), ("rx", 1, 4), ("rx", 1, 0), ("rx", 1, 5), ("mul", 0, 6), ("norm", 0, 14),
+    ("rx", 1, 10), ("rx", 0, 27), ("rx", 1, 6), ("norm", 0, 15), ("mul", 0, 2), ("mul", 0, 1), ("rx", 1, 9),
+    ("rx", 0, 25), ("rx", 0, 24), ("rx", 1, 2), ("rx", 1, 1), ("rx", 1, 8), ("mul", 1, 7), ("rx", 1, 3), ("dsum", 0, 0),
+    ("rx", 1, 11), ("mul", 0, 0), ("blk", 0, 0), ("blk", 0, 1), ("rx", 1, 21), ("blk", 0, 2), ("rx", 1, 12),
+    ("blk", 0, 3), ("rx", 1, 15), ("rx", 1, 19), ("rx", 1, 23), ("rx", 1, 17), ("blk", 0, 4), ("rx", 1, 7),
+    ("rx", 1, 13), ("rx", 1, 22), ("cmb", 0, 0), ("blk", 0, 5), ("rx", 1, 14), ("cmb", 0, 2), ("rx", 1, 18),
+    ("cmb", 0, 1), ("blk", 0, 6), ("cmb", 0, 3), ("cmb", 0, 4), ("rx", 1, 16), ("rx", 1, 20), ("mul", 1, 6),
+    ("mul", 1, 3), ("dboth", 0, 0), ("snd", 0, 15), ("rx", 1, 27), ("rx", 1, 25), ("cmb", 0, 5), ("snd", 0, 12),
+    ("rx", 1, 24), ("rx", 1, 26), ("mul", 1, 1), ("cmb", 0, 6), ("snd", 0, 17), ("mul", 1, 2), ("mul", 1, 4),
+    ("snd", 0, 21), ("mul", 1, 5), ("mul", 1, 0), ("blk", 1, 0), ("snd", 0, 8), ("snd", 0, 4), ("blk", 1, 1),
+    ("snd", 0, 0), ("snd", 0, 6), ("snd", 0, 10), ("blk", 1, 2), ("cmb", 1, 0), ("snd", 0, 5), ("blk", 1, 3),
+    ("blk", 1, 4), ("snd", 0, 9), ("cmb", 1, 1), ("cmb", 1, 2), ("blk", 0, 7), ("blk", 1, 5), ("snd", 1, 15),
+    ("snd", 1, 12), ("blk", 1, 6), ("cmb", 1, 3), ("cmb", 1, 4), ("blk", 1, 7), ("snd", 1, 17), ("snd", 0, 1),
+    ("snd", 1, 21), ("cmb", 1, 5), ("cmb", 1, 6), ("snd", 1, 1), ("snd", 1, 0), ("snd", 1, 10), ("snd", 1, 6),
+    ("cmb", 1, 7), ("upd", 0, 0), ("upd", 0, 1), ("cmb", 0, 7), ("snd", 1, 8), ("snd", 1, 4), ("snd", 1, 9),
+    ("upd", 0, 2), ("fin", 0, 2), ("snd", 1, 5), ("fin", 0, 1), ("fin", 0, 0), ("fin", 1, 1), ("fin", 0, 3),
+    ("upd", 0, 3), ("fin", 1, 0), ("fin", 1, 3), ("fin", 1, 2),
 )
 
 
@@ -113,6 +117,7 @@
     send_sem,
     recv_sem,
     load_sem,
+    ready_sem,
 ):
     r, f = lax.axis_index("replica"), lax.axis_index("fsdp")
     x_lo, y = r // 4, lax.rem(r, 4)
@@ -174,15 +179,28 @@
         return weights[g].at[pl.ds(pl.multiple_of((chip(block) * 2 + core) * BLOCK + first, 16), count)]
 
     barrier = pltpu.get_barrier_semaphore()
-    partners = [to_core, to["U"], to["D"], to["S"], to_side] + to_y
-    for device in partners:
+    for device in (to["S"], to["U"], to["D"], to_core):
         pl.semaphore_signal(barrier, inc=1, device_id=device, device_id_type=MESH)
-    pl.semaphore_wait(barrier, len(partners))
+
+    def greet(sem, towards_higher):
+        for k in (1, 2, 3):
+
+            @pl.when((y + k < 4) if towards_higher else (y + k >= 4))
+            def _():
+                pl.semaphore_signal(sem, inc=1, device_id=to_y[k - 1], device_id_type=MESH)
+
+        @pl.when(x_lo == (0 if towards_higher else 1))
+        def _():
+            pl.semaphore_signal(sem, inc=1, device_id=to_side, device_id_type=MESH)
+
+    greet(barrier, True)
+    pl.semaphore_wait(barrier, 4 + y + x_lo)
 
     load("own0", wo_in.at[0], weight(0, (0, 0), c))
     load("own1", wv_in.at[0], weight(1, (0, 0), c))
 
-    def load_rest():
+    def load_rest(_, __):
+        greet(ready_sem, False)
         load("dv", dv_in.at[0], scaled)
         load("cot", cot_in.at[0], cot)
         for k in range(TOK_PARTS):
@@ -195,14 +213,12 @@
     multiplied = [0, 0]
 
     def start(g, _):
-        own = {link: [k for k, m in enumerate(PLAN) if m[4] is None and m[0] == link] for link in "SUD"}
-        for i in range(4):
-            for link in "SUD":
-                k = own[link][i]
-                first, count = rows_of(g, PLAN[k][3])
-                piece = weights_in[g].at[0, pl.ds(first, count)]
-                send(g * GROUP + k, piece, weight(g, (0, 0), c, PLAN[k][3]), to[link])
         send(g * GROUP + COUNT + BLOCKS.index((0, 0)), weights_in[g].at[0], weight(g, (0, 0), c), to_core)
+
+    def own(g, k):
+        first, count = rows_of(g, PLAN[k][3])
+        piece = weights_in[g].at[0, pl.ds(first, count)]
+        send(g * GROUP + k, piece, weight(g, (0, 0), c, PLAN[k][3]), to[PLAN[k][0]])
 
     def rx(g, k):
         _, _, block, part, _ = PLAN[k]
@@ -299,6 +315,14 @@
             return 0
 
         lax.fori_loop(0, FRAG // 128, some, 0, unroll=4)
+
+    def dsend(_, __):
+        higher = 4 - y - x_lo
+
+        @pl.when(higher > 0)
+        def _():
+            pl.semaphore_wait(ready_sem, higher)
+
         for k in (1, 2, 3):
             send(DELTA + k - 1, seg(scaled, k), segs.at[k - 1], to_y[k - 1])
 
@@ -349,6 +373,8 @@
 
     tasks = {
         "start": start,
+        "own": own,
+        "load": load_rest,
         "rx": rx,
         "mul": mul,
         "blk": blk,
@@ -357,14 +383,13 @@
         "fin": fin,
         "norm": norm,
         "scale": scale,
+        "dsend": dsend,
         "dsum": dsum,
         "dboth": dboth,
         "upd": upd,
     }
     for name, g, k in ORDER:
         tasks[name](g, k)
-        if (name, g) == ("start", 0):
-            load_rest()
     for copy in sent:
         copy.wait_send()
 
@@ -406,6 +431,7 @@
             pltpu.SemaphoreType.DMA((MSGS,)),
             pltpu.SemaphoreType.DMA((MSGS,)),
             pltpu.SemaphoreType.DMA((TOK_PARTS + 6,)),
+            pltpu.SemaphoreType.REGULAR,
         ],
         compiler_params=pltpu.CompilerParams(
             collective_id=0, has_side_effects=True, vmem_limit_bytes=54 * 2**20

time: 72.3 us -> 69.7 us (0.964)
  Pallas kernels: 70.8 us -> 68.6 us
    pallas_call x1, Pallas kernels: 68.8 us -> 66.6 us  [per_device(): pl.pallas_call(kernel, out_shape=tuple((pltpu.VMEM(*shape) for shape in s...]
where the time goes in v3:
time: 69.7 us; the launch traced here: 69.4 us
  Pallas kernels  68.6 us (98%)
  between operations  0.8 us (1%)
    pallas_call x1, Pallas kernels, per_device(): pl.pallas_call(kernel, out_shape=tuple((pltpu.VMEM(*shape) for shape in s...  66.6 us
    pallas_call x1, Pallas kernels, per_device(): pl.pallas_call(hand_over, out_shape=tuple((jax.ShapeDtypeStruct(*shape) f...  2.05 us

profile of v3, /device:TPU:0, one launch (start us, length us, event | category | flops | bytes accessed | tf_op | source)
XLA Modules:
  0.0 69.4 jit_solution(16242978372125109213)
XLA Ops:
  0.6 66.6 %layer_and_outer_step.1 = (f32[1,256,512]{2,1,0:T(8,128)S(1)}, f32[1,256,512]{2,1,0:T(8,128)S(1)}, bf16[4096,128]{1,0:T(8,128)(2,1)S(1)}, f32[4096,128]{1,0:T(8,128)S(1)}) custom-call(bf16[1,1024,4096]{2,1,0:T(8,128)(2,1)} %tok_in.1, f32[1,4096]{1,0:T(1,128)} %bitcast.1, bf16[1,256,512]{2,1,0:T(8,128)(2,1)} %wv_in.1, bf16[1,256,512]{2,1,0:T(8,128)(2,1)} %wo_in.1, ...), custom_call_target="tpu_custom_call" | custom-call | tf_op jit(solution)/shard_map/layer_and_outer_step/pallas_call | solution.py:411
  67.2 2.0 %hand_over.1 = (f32[1,256,512]{2,1,0:T(8,128)}, f32[1,256,512]{2,1,0:T(8,128)}, bf16[4096,128]{1,0:T(8,128)(2,1)}, f32[4096,128]{1,0:T(8,128)}) custom-call(f32[1,256,512]{2,1,0:T(8,128)S(1)} %get-tuple-element.8.refs_0_, f32[1,256,512]{2,1,0:T(8,128)S(1)} %get-tuple-element.9.refs_1_, bf16[4096,128]{1,0:T(8,128)(2,1)S(1)} %get-tuple-element.10.refs_2_, ...), custom_call_target="tpu_custom_call" | custom-call | tf_op jit(solution)/shard_map/hand_over/pallas_call | solution.py:441

commit v4 on v3

--- a/solution.py
+++ b/solution.py
@@ -196,10 +196,10 @@
     greet(barrier, True)
     pl.semaphore_wait(barrier, 4 + y + x_lo)
 
-    load("own0", wo_in.at[0], weight(0, (0, 0), c))
-    load("own1", wv_in.at[0], weight(1, (0, 0), c))
 
     def load_rest(_, __):
+        load("own0", wo_in.at[0], weight(0, (0, 0), c))
+        load("own1", wv_in.at[0], weight(1, (0, 0), c))
         greet(ready_sem, False)
         load("dv", dv_in.at[0], scaled)
         load("cot", cot_in.at[0], cot)

time: 69.7 us -> 69.7 us (level)
  no operation moved by 1% of the time
where the time goes in v4:
time: 69.7 us; the launch traced here: 69.4 us
  Pallas kernels  68.6 us (98%)
  between operations  0.8 us (1%)
    pallas_call x1, Pallas kernels, per_device(): pl.pallas_call(kernel, out_shape=tuple((pltpu.VMEM(*shape) for shape in s...  66.6 us
    pallas_call x1, Pallas kernels, per_device(): pl.pallas_call(hand_over, out_shape=tuple((jax.ShapeDtypeStruct(*shape) f...  2.05 us

profile of v4, /device:TPU:0, one launch (start us, length us, event | category | flops | bytes accessed | tf_op | source)
XLA Modules:
  0.0 69.4 jit_solution(6507591179320992411)
XLA Ops:
  0.6 66.6 %layer_and_outer_step.1 = (f32[1,256,512]{2,1,0:T(8,128)S(1)}, f32[1,256,512]{2,1,0:T(8,128)S(1)}, bf16[4096,128]{1,0:T(8,128)(2,1)S(1)}, f32[4096,128]{1,0:T(8,128)S(1)}) custom-call(bf16[1,1024,4096]{2,1,0:T(8,128)(2,1)} %tok_in.1, f32[1,4096]{1,0:T(1,128)} %bitcast.1, bf16[1,256,512]{2,1,0:T(8,128)(2,1)} %wv_in.1, bf16[1,256,512]{2,1,0:T(8,128)(2,1)} %wo_in.1, ...), custom_call_target="tpu_custom_call" | custom-call | tf_op jit(solution)/shard_map/layer_and_outer_step/pallas_call | solution.py:411
  67.2 2.0 %hand_over.1 = (f32[1,256,512]{2,1,0:T(8,128)}, f32[1,256,512]{2,1,0:T(8,128)}, bf16[4096,128]{1,0:T(8,128)(2,1)}, f32[4096,128]{1,0:T(8,128)}) custom-call(f32[1,256,512]{2,1,0:T(8,128)S(1)} %get-tuple-element.8.refs_0_, f32[1,256,512]{2,1,0:T(8,128)S(1)} %get-tuple-element.9.refs_1_, bf16[4096,128]{1,0:T(8,128)(2,1)S(1)} %get-tuple-element.10.refs_2_, ...), custom_call_target="tpu_custom_call" | custom-call | tf_op jit(solution)/shard_map/hand_over/pallas_call | solution.py:441
